TPU v7x, 32 devices: a whole 2x2x4 slice. The times are simulated.
32 devices in a mesh: grp: 2 (over x), pix: 16 (over z, y, core).
Axes of the slice: x: 2, y: 2, z: 4, core: 2. Of those that a mesh axis runs over, the one named last changes fastest.
Arguments:
- fields: bfloat16 [2, 2, 128, 512, 512], P('grp', None, None, 'pix'), may hold values from -6 to 6
- lens_phase: float32 [512, 512], P('pix'), may hold values from -3.140625 to 3.140625
- occupancy: float32 [256], replicated, may hold values from 0.05 to 1
- focus_scale: float32 [256], replicated, may hold values from 0.5 to 1.5
- assignment: int32 [256], replicated, may hold values from 0 to 255, each once
- start_basis: float32 [2, 256, 128], replicated, may hold values from -6 to 6
Outputs:
- coherent_modes: bfloat16 [2, 128, 512, 512], P(None, None, 'pix', 'grp')
- relative_power: float32 [128], replicated
Inputs may be any that keep to these rules, and one draw needn't show every extreme that they name: `assignment`: each electron is carried by exactly one wavefront slot.
All inputs are finite; a program needn't handle non-finite values.
Results may differ from a plain program's by a relative error of at most 0.0018.
The roundings to bfloat16 on the way count: a program that leaves them out, or rounds other values in their place, can miss the bound.
Values may be sent and summed in bfloat16 or wider, within the bound.
A program may use at most 128 MiB of HBM per device.

v0:
```python
import math

import jax
import jax.numpy as jnp
from jax import lax
from jax.sharding import PartitionSpec as P

NROW = 512
NCOL = 512
STEPS = 2


def partner_2(array, axis, apart):
    return lax.ppermute(array, axis, [(i, i ^ 1 << apart) for i in range(lax.axis_size(axis))])


def dft_tables(length):
    index = jnp.arange(length, dtype=jnp.int32)
    product = index[:, None] * index[None, :] % length
    angle = product.astype(jnp.float32) * (2.0 * math.pi / length)
    factor = 1.0 / math.sqrt(length)
    return (
        (jnp.cos(angle) * factor).astype(jnp.bfloat16),
        (jnp.sin(angle) * factor).astype(jnp.bfloat16),
    )


def local(fields, lens_phase, occupancy, focus_scale, assignment, start_basis):
    highest = lax.Precision.HIGHEST
    local_fields = fields[0]
    modes = local_fields.shape[1]
    group_index = lax.axis_index("grp")
    electron = lax.dynamic_slice_in_dim(assignment, group_index * modes, modes)
    choose = (
        electron[:, None] == jnp.arange(assignment.shape[0], dtype=jnp.int32)[None, :]
    ).astype(jnp.float32)
    amplitude = jnp.sqrt(jnp.sum(choose * occupancy[None, :], axis=1))[:, None, None]
    chromatic = jnp.sum(choose * focus_scale[None, :], axis=1)
    angle = chromatic[:, None, None] * lens_phase[None]
    cosine = jnp.cos(angle)
    sine = jnp.sin(angle)
    field_re = local_fields[0].astype(jnp.float32)
    field_im = local_fields[1].astype(jnp.float32)
    phased = jnp.stack(
        [
            amplitude * (field_re * cosine - field_im * sine),
            amplitude * (field_re * sine + field_im * cosine),
        ]
    ).astype(jnp.bfloat16)
    cos_cols, sin_cols = dft_tables(lens_phase.shape[1])
    col_cos = jnp.einsum("zmrc,ck->zmkr", phased, cos_cols, preferred_element_type=jnp.float32)
    col_sin = jnp.einsum("zmrc,ck->zmkr", phased, sin_cols, preferred_element_type=jnp.float32)
    across = jnp.stack([col_cos[0] + col_sin[1], col_cos[1] - col_sin[0]]).astype(jnp.bfloat16)
    full_rows = across.shape[3] * lax.axis_size("pix")
    cos_rows, sin_rows = dft_tables(full_rows)
    pieces = lax.all_to_all(across, "pix", split_axis=2, concat_axis=3, tiled=True)
    row_cos = jnp.dot(pieces, cos_rows, preferred_element_type=jnp.float32)
    row_sin = jnp.dot(pieces, sin_rows, preferred_element_type=jnp.float32)
    focal = jnp.stack([row_cos[0] + row_sin[1], row_cos[1] - row_sin[0]]).astype(jnp.bfloat16)
    stack_size = modes * lax.axis_size("grp")
    half_rows = full_rows // lax.axis_size("grp")
    partner = partner_2(focal, "grp", 0)
    leading = jnp.where(group_index == 0, focal, partner)
    trailing = jnp.where(group_index == 0, partner, focal)
    stacked = jnp.concatenate([leading, trailing], axis=1)
    flat = stacked.reshape(2, stack_size, -1)
    blocks = jnp.einsum("xap,ybp->xyab", flat, flat, preferred_element_type=jnp.float32)
    local_re = blocks[0, 0] + blocks[1, 1]
    local_im = blocks[0, 1] - blocks[1, 0]
    gram_re, gram_im = lax.psum((local_re, local_im), "pix")
    owned = lax.dynamic_slice_in_dim(stacked, group_index * half_rows, half_rows, 3)
    basis_re = start_basis[0]
    basis_im = start_basis[1]
    for iteration in range(STEPS):
        image_re = jnp.dot(gram_re, basis_re, precision=highest) - jnp.dot(
            gram_im, basis_im, precision=highest
        )
        image_im = jnp.dot(gram_re, basis_im, precision=highest) + jnp.dot(
            gram_im, basis_re, precision=highest
        )
        column_norm = jnp.sqrt(jnp.sum(image_re * image_re + image_im * image_im, axis=0) + 1e-06)
        basis_re = image_re / column_norm[None, :]
        basis_im = image_im / column_norm[None, :]
    rounded = jnp.stack([basis_re, basis_im]).astype(jnp.bfloat16)
    rank = rounded.shape[2]
    owned_flat = owned.reshape(2, stack_size, -1)
    products = jnp.einsum("xsk,ysp->xykp", rounded, owned_flat, preferred_element_type=jnp.float32)
    mode_re = products[0, 0] - products[1, 1]
    mode_im = products[0, 1] + products[1, 0]
    coeff_re = rounded[0].astype(jnp.float32)
    coeff_im = rounded[1].astype(jnp.float32)
    weighted_re = jnp.dot(gram_re, coeff_re, precision=highest) - jnp.dot(
        gram_im, coeff_im, precision=highest
    )
    weighted_im = jnp.dot(gram_re, coeff_im, precision=highest) + jnp.dot(
        gram_im, coeff_re, precision=highest
    )
    energy = jnp.sum(coeff_re * weighted_re + coeff_im * weighted_im, axis=0)
    trace = jnp.sum(jnp.diagonal(gram_re))
    relative_power = energy * stack_size / trace
    inverse = lax.rsqrt(energy / (NROW * NCOL) + 1e-06)
    coherent_modes = (jnp.stack([mode_re, mode_im]) * inverse[None, :, None]).astype(jnp.bfloat16)
    return (coherent_modes.reshape(2, rank, owned.shape[2], owned.shape[3]), relative_power)


def solution(mesh):
    in_specs = (P("grp", None, None, "pix", None), P("pix", None), P(), P(), P(), P())
    out_specs = (P(None, None, "pix", "grp"), P())
    return jax.shard_map(local, mesh=mesh, in_specs=in_specs, out_specs=out_specs, check_vma=False)
```

profile of v0, /device:TPU:0, one launch (start us, length us, event | category | flops | bytes accessed | tf_op | source)
XLA Modules:
  0.0 718.5 jit_solution(4285038648514681702)
XLA Ops:
  7.2 0.0 all-reduce.3.cloned.1.call-start
  7.2 0.8 dynamic_slice.6
  8.0 0.9 select_reduce_fusion.1
  8.9 0.0 copy-start.6
  8.9 3.8 fusion.82
  12.7 37.1 %fusion.9 = (bf16[1,128,32,512]{3,1,2,0:T(8,128)(2,1)S(1)}, bf16[1,128,32,512]{3,1,2,0:T(8,128)(2,1)S(1)}) fusion(f32[32,512]{1,0:T(8,128)S(1)} %copy-done.6, f32[128]{0:T(128)S(1)} %get-tuple-element.3, f32[128]{0:T(128)S(1)} %sqrt.21, bf16[1,1,128,32,512]{4,3,2,1,0:T(8,128)(2,1)S(1)} %get-tuple-element.17, ...), kind=kLoop, calls=%fused_computation.16 | loop fusion | flops 27262976 | bytes 16843776 | tf_op jit(solution)/shard_map/convert.10
  49.8 14.0 %convolution_bitcast_fusion.2 = f32[2,128,512,32]{1,2,3,0:T(8,128)} fusion(bf16[1,128,32,512]{3,1,2,0:T(8,128)(2,1)S(1)} %get-tuple-element.15, bf16[1,128,32,512]{3,1,2,0:T(8,128)(2,1)S(1)} %get-tuple-element.14), kind=kOutput, calls=%fused_computation.37 | convolution fusion | flops 4315938816 | bytes 25165824 | tf_op jit(solution)/shard_map/zmrc,ck->zmkr/dot_general | solution.py:51
  63.8 14.4 %convolution_bitcast_fusion.1 = f32[2,128,512,32]{1,2,3,0:T(8,128)} fusion(bf16[1,128,32,512]{3,1,2,0:T(8,128)(2,1)S(1)} %get-tuple-element.15, bf16[1,128,32,512]{3,1,2,0:T(8,128)(2,1)S(1)} %get-tuple-element.14), kind=kOutput, calls=%fused_computation.36 | convolution fusion | flops 4315938816 | bytes 25165824 | tf_op jit(solution)/shard_map/zmrc,ck->zmkr/dot_general | solution.py:52
  78.2 13.9 %fusion.17 = (bf16[1,128,512,32]{1,2,3,0:T(8,128)(2,1)S(1)}, bf16[1,128,512,32]{1,2,3,0:T(8,128)(2,1)}) fusion(f32[2,128,512,32]{1,2,3,0:T(8,128)} %convolution_bitcast_fusion.1, f32[2,128,512,32]{1,2,3,0:T(8,128)} %convolution_bitcast_fusion.2), kind=kLoop, calls=%fused_computation.28 | loop fusion | flops 8388608 | bytes 41943040 | tf_op jit(solution)/shard_map/convert.8
  92.1 6.2 pad_maximum_fusion.3
  98.3 12.0 %copy.51 = bf16[2,128,512,32]{1,3,0,2:T(8,128)(2,1)} copy(bf16[2,128,512,32]{1,2,3,0:T(8,128)(2,1)} %pad_maximum_fusion.3) | data formatting | bytes 16777216 | tf_op jit(solution)/shard_map/stack | solution.py:53
  110.3 189.8 %all_to_all.18 = bf16[2,128,512,32]{1,3,0,2:T(8,128)(2,1)} all-to-all(bf16[2,128,512,32]{1,3,0,2:T(8,128)(2,1)} %copy.51), channel_id=1, replica_groups=mesh['grp'=2,'pix'=16] {'pix'}, dimensions={2} | all-to-all | bytes 16777216 | tf_op jit(solution)/shard_map/all_to_all | solution.py:56
  300.1 9.2 %copy.53 = bf16[2,128,32,16,32]{1,4,3,2,0:T(8,128)(2,1)} copy(bf16[2,128,32,16,32]{1,4,0,2,3:T(8,128)(2,1)} %bitcast.105) | data formatting | bytes 16777216 | tf_op jit(solution)/shard_map/all_to_all | solution.py:56
  309.3 15.4 %fusion.36 = f32[2,128,32,512]{3,1,2,0:T(8,128)} fusion(bf16[2,128,32,512]{1,3,2,0:T(8,128)(2,1)} %bitcast.102), kind=kOutput, calls=%fused_computation.66 | convolution fusion | flops 4299161600 | bytes 25165824 | tf_op jit(solution)/shard_map/dot_general | solution.py:58
  324.7 12.0 %fusion.39 = f32[2,128,32,512]{3,1,2,0:T(8,128)} fusion(bf16[2,128,32,512]{1,3,2,0:T(8,128)(2,1)S(1)} %bitcast.103), kind=kOutput, calls=%fused_computation.67 | convolution fusion | flops 4299161600 | bytes 25165824 | tf_op jit(solution)/shard_map/dot_general | solution.py:57
  336.7 14.3 %fusion.15 = (bf16[1,128,32,512]{3,1,2,0:T(8,128)(2,1)S(1)}, bf16[1,128,32,512]{3,1,2,0:T(8,128)(2,1)}) fusion(f32[2,128,32,512]{3,1,2,0:T(8,128)} %fusion.36, f32[2,128,32,512]{3,1,2,0:T(8,128)} %fusion.39), kind=kLoop, calls=%fused_computation.24 | loop fusion | flops 8388608 | bytes 41943040 | tf_op jit(solution)/shard_map/convert.6
  351.0 7.7 %pad_maximum_fusion.4 = bf16[2,128,32,512]{3,1,2,0:T(8,128)(2,1)} fusion(bf16[1,128,32,512]{3,1,2,0:T(8,128)(2,1)} %get-tuple-element.7, bf16[1,128,32,512]{3,1,2,0:T(8,128)(2,1)S(1)} %get-tuple-element.6), kind=kLoop, calls=%fused_computation.31 | loop fusion | flops 4194304 | bytes 16777216 | tf_op jit(solution)/shard_map/stack | solution.py:59
  358.7 1.5 collective-permute-start
  360.2 182.0 %collective-permute-done = bf16[2,128,32,512]{3,1,2,0:T(8,128)(2,1)} collective-permute-done((bf16[2,128,32,512]{3,1,2,0:T(8,128)(2,1)}, bf16[2,128,32,512]{3,1,2,0:T(8,128)(2,1)}, u32[]{:S(2)}, u32[]{:S(2)}) %collective-permute-start) | collective-permute-done | bytes 8388640 | tf_op jit(solution)/shard_map/ppermute | solution.py:14
  542.1 6.3 broadcast_select_fusion
  548.5 0.0 copy-start.2
  548.5 0.0 copy-start.3
  548.5 12.3 %fusion.19 = f32[2,2,256,256]{2,3,0,1:T(8,128)S(1)} fusion(bf16[2,128,32,512]{3,1,2,0:T(8,128)(2,1)S(1)} %get-tuple-element.12, bf16[2,128,32,512]{3,1,2,0:T(8,128)(2,1)S(1)} %get-tuple-element.13), kind=kOutput, calls=%fused_computation.45 | convolution fusion | flops 8657043456 | bytes 17825792 | tf_op jit(solution)/shard_map/xap,ybp->xyab/dot_general | solution.py:67
  560.8 0.8 fusion.42
  561.7 0.0 all-reduce.3.cloned.1.call-update
  561.7 7.8 %fusion.13 = bf16[2,256,32,256]{3,1,2,0:T(8,128)(2,1)} fusion(s32[]{:T(128)S(6)} %select_n.42, bf16[2,128,32,512]{3,1,2,0:T(8,128)(2,1)} %copy-done.3, bf16[2,128,32,512]{3,1,2,0:T(8,128)(2,1)} %copy-done.2), kind=kLoop, calls=%fused_computation.20 | loop fusion | flops 16777216 | bytes 25165828 | tf_op jit(solution)/shard_map/concatenate | solution.py:65
  569.5 12.2 %copy.56 = bf16[2,256,32,256]{1,3,2,0:T(8,128)(2,1)} copy(bf16[2,256,32,256]{3,1,2,0:T(8,128)(2,1)} %fusion.13) | data formatting | bytes 16777216 | tf_op jit(solution)/shard_map/dynamic_slice | solution.py:71
  581.7 70.7 %all-reduce.3.cloned.1.call-done = (f32[256,256]{0,1:T(8,128)}, f32[256,256]{0,1:T(8,128)}) async-done(((f32[256,256]{0,1:T(8,128)}, f32[256,256]{0,1:T(8,128)}), (f32[256,256]{0,1:T(8,128)}, f32[256,256]{0,1:T(8,128)})) %all-reduce.3.cloned.1.call-update) | async-done | bytes 524304 | tf_op jit(solution)/shard_map/psum | solution.py:70
  652.5 1.5 fusion.50
  654.0 1.5 fusion.46
  655.6 1.5 convolution_subtract_fusion.1
  657.1 1.6 add_reduce_fusion.1
  658.7 1.5 fusion.56
  660.2 1.5 fusion.57
  661.8 1.5 convolution_subtract_fusion
  663.3 1.6 add_reduce_fusion
  664.9 1.3 fusion.84
  666.3 1.3 fusion.83
  667.6 1.3 fusion.26
  669.0 2.6 gather_fusion
  671.6 11.5 %convolution_bitcast_fusion = f32[2,2,128,8192]{2,3,0,1:T(8,128)} fusion(bf16[2,256,8192,1]{1,2,3,0:T(8,128)(2,1)} %bitcast.104, bf16[1,256,128]{2,1,0:T(8,128)(2,1)S(1)} %bitcast.110, bf16[1,256,128]{2,1,0:T(8,128)(2,1)S(1)} %bitcast.109), kind=kOutput, calls=%fused_computation.7 | convolution fusion | flops 2147745792 | bytes 25296896 | tf_op jit(solution)/shard_map/xsk,ysp->xykp/dot_general | solution.py:87
  683.1 10.0 %slice_subtract_fusion.2 = (f32[1,1,128,8192]{2,3,0,1:T(8,128)}, f32[1,1,128,8192]{2,3,0,1:T(8,128)}) fusion(f32[2,2,128,8192]{2,3,0,1:T(8,128)} %convolution_bitcast_fusion), kind=kLoop, calls=%fused_computation.39 | loop fusion | flops 2097152 | bytes 25165824 | tf_op jit(solution)/shard_map/sub | solution.py:88
  693.1 5.5 copy.57
  698.6 5.5 copy.58
  704.1 0.4 fusion.27
  704.5 0.6 reduce_sum.59
  705.1 1.2 multiply_divide_fusion
  706.3 5.2 fusion.18
  (16 shorter events, 0.1 us)
Async XLA Ops:
  7.2 645.3 %all-reduce.3.cloned.1.call-start = ((), (), s32[]{:S(2)}) async-start(), calls=%async_computation.1 | async-start | bytes 1048576 | tf_op jit(solution)/shard_map/psum | solution.py:70
  8.9 3.9 copy-start.6
  309.3 15.4 %copy-start = (bf16[2,128,32,16,32]{1,4,3,2,0:T(8,128)(2,1)S(1)}, bf16[2,128,32,16,32]{1,4,3,2,0:T(8,128)(2,1)}, u32[]{:S(2)}) copy-start(bf16[2,128,32,16,32]{1,4,3,2,0:T(8,128)(2,1)} %copy.53) | copy-start | bytes 25165828
  351.0 7.7 %copy-start.1 = (bf16[1,128,32,512]{3,1,2,0:T(8,128)(2,1)}, bf16[1,128,32,512]{3,1,2,0:T(8,128)(2,1)S(1)}, u32[]{:S(2)}) copy-start(bf16[1,128,32,512]{3,1,2,0:T(8,128)(2,1)S(1)} %get-tuple-element.6) | copy-start | bytes 12582916
  358.7 183.5 %collective-permute-start = (bf16[2,128,32,512]{3,1,2,0:T(8,128)(2,1)}, bf16[2,128,32,512]{3,1,2,0:T(8,128)(2,1)}, u32[]{:S(2)}, u32[]{:S(2)}) collective-permute-start(bf16[2,128,32,512]{3,1,2,0:T(8,128)(2,1)} %pad_maximum_fusion.4), channel_id=1, source_target_pairs={{0,16},{16,0},{1,17},{17,1},{2,18},{18,2},{3,19},{19,3},{4,20},{20... | collective-permute-start | bytes 25165832 | tf_op jit(solution)/shard_map/ppermute | solution.py:14
  548.5 12.3 %copy-start.2 = (bf16[2,128,32,512]{3,1,2,0:T(8,128)(2,1)}, bf16[2,128,32,512]{3,1,2,0:T(8,128)(2,1)S(1)}, u32[]{:S(2)}) copy-start(bf16[2,128,32,512]{3,1,2,0:T(8,128)(2,1)S(1)} %get-tuple-element.12) | copy-start | bytes 25165828
  548.5 12.3 %copy-start.3 = (bf16[2,128,32,512]{3,1,2,0:T(8,128)(2,1)}, bf16[2,128,32,512]{3,1,2,0:T(8,128)(2,1)S(1)}, u32[]{:S(2)}) copy-start(bf16[2,128,32,512]{3,1,2,0:T(8,128)(2,1)S(1)} %get-tuple-element.13) | copy-start | bytes 25165828
  569.5 83.0 %copy-start.5 = (f32[2,256,128]{2,1,0:T(8,128)S(1)}, f32[2,256,128]{2,1,0:T(8,128)}, u32[]{:S(2)}) copy-start(f32[2,256,128]{2,1,0:T(8,128)} %param.11) | copy-start | bytes 786436
  693.1 11.0 %copy-start.4 = (f32[256,256]{0,1:T(8,128)S(1)}, f32[256,256]{0,1:T(8,128)}, u32[]{:S(2)}) copy-start(f32[256,256]{0,1:T(8,128)} %get-tuple-element.5) | copy-start | bytes 786436
Sparse Core Ops, SparseCore 0:
  561.8 90.6 all-reduce.2
where the time goes:
time: 724 us; the launch traced here: 719 us
  waiting for transfers between devices  253 us (35%)
  blocking collectives  190 us (26%)
  other arithmetic  112 us (15%)
  matrix products  96.3 us (13%)
  local copies, waits for them, and re-layouts  51.7 us (7%)
  between operations  14.4 us (2%)
    all_to_all x1, blocking collectives, local(): lax.all_to_all(across, 'pix', split_axis=2, concat_axis=3, tiled=True)  190 us
    ppermute x1, waiting for transfers between devices, partner_2(): lax.ppermute(array, axis, [(i, i ^ 1 << apart) for i in range(lax.axis_si...  182 us
    psum x1, waiting for transfers between devices, local(): gram_re, gram_im = lax.psum((local_re, local_im), 'pix')  70.7 us
    another operation x3, other arithmetic  65.4 us
    dot_general x1, matrix products, local(): row_sin = jnp.dot(pieces, sin_rows, preferred_element_type=jnp.float32)  15.4 us
  transfers between devices with their start and end apart: 2, of which 2 were waited for; matrix products, arithmetic and copies ran while one was open for 3% of the time, Pallas kernels for 0%

commit v1 on v0

--- a/solution.py
+++ b/solution.py
@@ -54,21 +54,29 @@
     full_rows = across.shape[3] * lax.axis_size("pix")
     cos_rows, sin_rows = dft_tables(full_rows)
     pieces = lax.all_to_all(across, "pix", split_axis=2, concat_axis=3, tiled=True)
-    row_cos = jnp.dot(pieces, cos_rows, preferred_element_type=jnp.float32)
-    row_sin = jnp.dot(pieces, sin_rows, preferred_element_type=jnp.float32)
-    focal = jnp.stack([row_cos[0] + row_sin[1], row_cos[1] - row_sin[0]]).astype(jnp.bfloat16)
+    half_rows = full_rows // lax.axis_size("grp")
+    cos_rows = jnp.roll(cos_rows, -group_index * half_rows, axis=1)
+    sin_rows = jnp.roll(sin_rows, -group_index * half_rows, axis=1)
+
+    def row_transform(first):
+        cos_part = cos_rows[:, first:first + half_rows]
+        sin_part = sin_rows[:, first:first + half_rows]
+        row_cos = jnp.dot(pieces, cos_part, preferred_element_type=jnp.float32)
+        row_sin = jnp.dot(pieces, sin_part, preferred_element_type=jnp.float32)
+        return jnp.stack([row_cos[0] + row_sin[1], row_cos[1] - row_sin[0]]).astype(jnp.bfloat16)
+
     stack_size = modes * lax.axis_size("grp")
-    half_rows = full_rows // lax.axis_size("grp")
-    partner = partner_2(focal, "grp", 0)
-    leading = jnp.where(group_index == 0, focal, partner)
-    trailing = jnp.where(group_index == 0, partner, focal)
-    stacked = jnp.concatenate([leading, trailing], axis=1)
-    flat = stacked.reshape(2, stack_size, -1)
+    partner = partner_2(row_transform(half_rows), "grp", 0)
+    owned = jnp.concatenate([row_transform(0), partner], axis=1)
+    flat = owned.reshape(2, stack_size, -1)
     blocks = jnp.einsum("xap,ybp->xyab", flat, flat, preferred_element_type=jnp.float32)
     local_re = blocks[0, 0] + blocks[1, 1]
     local_im = blocks[0, 1] - blocks[1, 0]
-    gram_re, gram_im = lax.psum((local_re, local_im), "pix")
-    owned = lax.dynamic_slice_in_dim(stacked, group_index * half_rows, half_rows, 3)
+
+    def ordered(block):
+        return jnp.where(group_index == 0, block, jnp.roll(block, (modes, modes), (0, 1)))
+
+    gram_re, gram_im = lax.psum((ordered(local_re), ordered(local_im)), ("grp", "pix"))
     basis_re = start_basis[0]
     basis_im = start_basis[1]
     for iteration in range(STEPS):
@@ -83,8 +91,9 @@
         basis_im = image_im / column_norm[None, :]
     rounded = jnp.stack([basis_re, basis_im]).astype(jnp.bfloat16)
     rank = rounded.shape[2]
+    local_rounded = jnp.where(group_index == 0, rounded, jnp.roll(rounded, modes, 1))
     owned_flat = owned.reshape(2, stack_size, -1)
-    products = jnp.einsum("xsk,ysp->xykp", rounded, owned_flat, preferred_element_type=jnp.float32)
+    products = jnp.einsum("xsk,ysp->xykp", local_rounded, owned_flat, preferred_element_type=jnp.float32)
     mode_re = products[0, 0] - products[1, 1]
     mode_im = products[0, 1] + products[1, 0]
     coeff_re = rounded[0].astype(jnp.float32)

time: 724 us -> 622 us (0.86)
  blocking collectives: 190 us -> 0 us
  waiting for transfers between devices: 253 us -> 368 us
  matrix products: 96.3 us -> 78.6 us
  other arithmetic: 112 us -> 94.8 us
  starting transfers between devices: 1.53 us -> 8.97 us
    all_to_all x1 -> x0, blocking collectives: 190 us -> none  [local(): lax.all_to_all(across, 'pix', split_axis=2, concat_axis=3, tiled=True)]
    all_to_all x0 -> x1, waiting for transfers between devices: none -> 142 us  [local(): lax.all_to_all(across, 'pix', split_axis=2, concat_axis=3, tiled=True)]
    ppermute x1, waiting for transfers between devices: 182 us -> 78.9 us  [partner_2(): lax.ppermute(array, axis, [(i, i ^ 1 << apart) for i in range(lax.axis_si...]
    psum x1, waiting for transfers between devices: 70.7 us -> 147 us  [local(): lax.psum((ordered(local_re), ordered(local_im)), ('grp', 'pix'))]
    another operation x4 -> x6, other arithmetic: 73 us -> 57.3 us
    dynamic_slice x1 -> x0, local copies, waits for them, and re-layouts: 12.2 us -> none  [local(): lax.dynamic_slice_in_dim(stacked, group_index * half_rows, half_rows, 3)]
    concatenate x0 -> x1, local copies, waits for them, and re-layouts: none -> 12.2 us  [local(): owned = jnp.concatenate([row_transform(0), partner], axis=1)]
    convert_element_type x0 -> x2, other arithmetic: none -> 8.18 us  [the longest x1 4.21 us: dft_tables(): (jnp.sin(angle) * factor).astype(jnp.bfloat16)]
  transfers between devices with their start and end apart: 2 -> 3, of which waited for: 2 -> 3; matrix products, arithmetic and copies ran while one was open for 3% -> 6% of each run, Pallas kernels for 0% -> 0%
where the time goes in v1:
time: 622 us; the launch traced here: 617 us
  waiting for transfers between devices  368 us (59%)
  other arithmetic  94.8 us (15%)
  matrix products  78.6 us (13%)
  local copies, waits for them, and re-layouts  51.7 us (8%)
  between operations  14.6 us (2%)
  starting transfers between devices  8.97 us (1%)
    psum x1, waiting for transfers between devices, local(): lax.psum((ordered(local_re), ordered(local_im)), ('grp', 'pix'))  147 us
    all_to_all x1, waiting for transfers between devices, local(): lax.all_to_all(across, 'pix', split_axis=2, concat_axis=3, tiled=True)  142 us
    ppermute x1, waiting for transfers between devices, partner_2(): lax.ppermute(array, axis, [(i, i ^ 1 << apart) for i in range(lax.axis_si...  78.9 us
    another operation x4, other arithmetic  55 us
    dot_general x1, matrix products, local(): jnp.einsum('zmrc,ck->zmkr', phased, sin_cols, preferred_element_type=jnp....  14.2 us
    dot_general x1, matrix products, local(): jnp.einsum('zmrc,ck->zmkr', phased, cos_cols, preferred_element_type=jnp....  14 us
  transfers between devices with their start and end apart: 3, of which 3 were waited for; matrix products, arithmetic and copies ran while one was open for 6% of the time, Pallas kernels for 0%

profile of v1, /device:TPU:0, one launch (start us, length us, event | category | flops | bytes accessed | tf_op | source)
XLA Modules:
  0.0 616.9 jit_solution(5536376364410026706)
XLA Ops:
  7.2 0.8 dynamic_slice.6
  7.9 0.9 select_reduce_fusion.1
  8.8 3.8 fusion.84
  12.7 37.5 %fusion.6 = (bf16[1,128,32,512]{3,1,2,0:T(8,128)(2,1)S(1)}, bf16[1,128,32,512]{3,1,2,0:T(8,128)(2,1)S(1)}) fusion(f32[32,512]{1,0:T(8,128)S(1)} %copy-done.3, f32[128]{0:T(128)S(1)} %get-tuple-element.4, f32[128]{0:T(128)S(1)} %sqrt.21, bf16[1,1,128,32,512]{4,3,2,1,0:T(8,128)(2,1)S(1)} %get-tuple-element.18, ...), kind=kLoop, calls=%fused_computation.10 | loop fusion | flops 27262976 | bytes 16843776 | tf_op jit(solution)/shard_map/convert.12
  50.1 14.0 %convolution_bitcast_fusion.2 = f32[2,128,512,32]{1,2,3,0:T(8,128)} fusion(bf16[1,128,32,512]{3,1,2,0:T(8,128)(2,1)S(1)} %get-tuple-element.16, bf16[1,128,32,512]{3,1,2,0:T(8,128)(2,1)S(1)} %get-tuple-element.15), kind=kOutput, calls=%fused_computation.27 | convolution fusion | flops 4315938816 | bytes 25165824 | tf_op jit(solution)/shard_map/zmrc,ck->zmkr/dot_general | solution.py:51
  64.1 14.2 %convolution_bitcast_fusion.1 = f32[2,128,512,32]{1,2,3,0:T(8,128)} fusion(bf16[1,128,32,512]{3,1,2,0:T(8,128)(2,1)S(1)} %get-tuple-element.16, bf16[1,128,32,512]{3,1,2,0:T(8,128)(2,1)S(1)} %get-tuple-element.15), kind=kOutput, calls=%fused_computation.26 | convolution fusion | flops 4315938816 | bytes 25165824 | tf_op jit(solution)/shard_map/zmrc,ck->zmkr/dot_general | solution.py:52
  78.3 13.9 %fusion.11 = (bf16[1,128,512,32]{1,2,3,0:T(8,128)(2,1)S(1)}, bf16[1,128,512,32]{1,2,3,0:T(8,128)(2,1)}) fusion(f32[2,128,512,32]{1,2,3,0:T(8,128)} %convolution_bitcast_fusion.1, f32[2,128,512,32]{1,2,3,0:T(8,128)} %convolution_bitcast_fusion.2), kind=kLoop, calls=%fused_computation.17 | loop fusion | flops 8388608 | bytes 41943040 | tf_op jit(solution)/shard_map/convert.10
  92.2 6.2 %pad_maximum_fusion.1 = bf16[2,128,512,32]{1,2,3,0:T(8,128)(2,1)} fusion(bf16[1,128,512,32]{1,2,3,0:T(8,128)(2,1)} %get-tuple-element.8, bf16[1,128,512,32]{1,2,3,0:T(8,128)(2,1)S(1)} %get-tuple-element.7), kind=kLoop, calls=%fused_computation.19 | loop fusion | flops 4194304 | bytes 16777216 | tf_op jit(solution)/shard_map/stack | solution.py:53
  98.4 12.0 %copy.69 = bf16[2,128,512,32]{1,3,0,2:T(8,128)(2,1)} copy(bf16[2,128,512,32]{1,2,3,0:T(8,128)(2,1)} %pad_maximum_fusion.1) | data formatting | bytes 16777216 | tf_op jit(solution)/shard_map/stack | solution.py:53
  110.4 7.4 %all-to-all-start = ((bf16[2,128,512,32]{1,3,0,2:T(8,128)(2,1)}), bf16[2,128,512,32]{1,3,0,2:T(8,128)(2,1)}, u32[]{:S(2)}, u32[]{:S(2)}) async-start(bf16[2,128,512,32]{1,3,0,2:T(8,128)(2,1)} %copy.69), calls=%async_computation | async-start | bytes 16777216 | tf_op jit(solution)/shard_map/all_to_all | solution.py:56
  117.9 4.2 multiply_convert_fusion
  122.1 4.0 multiply_convert_fusion.1
  126.5 142.0 %all-to-all-done = bf16[2,128,512,32]{1,3,0,2:T(8,128)(2,1)} async-done(((bf16[2,128,512,32]{1,3,0,2:T(8,128)(2,1)}), bf16[2,128,512,32]{1,3,0,2:T(8,128)(2,1)}, u32[]{:S(2)}, u32[]{:S(2)}) %all-to-all-start) | async-done | bytes 8388640 | tf_op jit(solution)/shard_map/all_to_all | solution.py:56
  268.5 9.2 %copy.71 = bf16[2,128,32,16,32]{1,4,3,2,0:T(8,128)(2,1)} copy(bf16[2,128,32,16,32]{1,4,0,2,3:T(8,128)(2,1)} %bitcast.10) | data formatting | bytes 16777216 | tf_op jit(solution)/shard_map/all_to_all | solution.py:56
  277.8 5.9 fusion.45
  283.7 2.4 fusion.44
  286.1 2.0 fusion.17
  288.1 2.4 pad_maximum_fusion.5
  290.5 1.5 collective-permute-start
  292.0 5.8 fusion.46
  297.7 5.8 fusion.47
  303.5 1.6 fusion.19
  305.1 78.9 %collective-permute-done = bf16[2,128,32,256]{3,1,2,0:T(8,128)(2,1)} collective-permute-done((bf16[2,128,32,256]{3,1,2,0:T(8,128)(2,1)}, bf16[2,128,32,256]{3,1,2,0:T(8,128)(2,1)}, u32[]{:S(2)}, u32[]{:S(2)}) %collective-permute-start) | collective-permute-done | bytes 4194336 | tf_op jit(solution)/shard_map/ppermute | solution.py:14
  384.0 3.1 pad_maximum_fusion.2
  387.2 4.5 fusion.20
  391.9 0.8 fusion.40
  392.7 0.8 fusion.42
  393.5 12.2 %copy.76 = bf16[2,256,32,256]{1,3,2,0:T(8,128)(2,1)} copy(bf16[2,256,32,256]{3,1,2,0:T(8,128)(2,1)} %copy-done) | data formatting | bytes 16777216 | tf_op jit(solution)/shard_map/concatenate | solution.py:70
  405.7 147.3 %all-reduce.3.cloned.1.call-done = (f32[256,256]{1,0:T(8,128)}, f32[256,256]{1,0:T(8,128)}) async-done(((f32[256,256]{1,0:T(8,128)}, f32[256,256]{1,0:T(8,128)}), (f32[256,256]{1,0:T(8,128)}, f32[256,256]{1,0:T(8,128)})) %all-reduce.3.cloned.1.call-update) | async-done | bytes 524304 | tf_op jit(solution)/shard_map/psum | solution.py:79
  553.1 1.3 fusion.60
  554.4 1.3 fusion.56
  555.7 1.3 convolution_subtract_fusion.1
  557.1 1.3 add_reduce_fusion.1
  558.4 1.3 fusion.69
  559.8 1.3 fusion.70
  561.1 1.3 convolution_subtract_fusion
  562.5 1.4 add_reduce_fusion
  563.9 1.2 fusion.86
  565.1 1.2 fusion.85
  566.3 1.2 fusion.27
  567.6 2.6 gather_fusion
  570.2 11.5 %convolution_bitcast_fusion = f32[2,2,128,8192]{2,3,0,1:T(8,128)} fusion(bf16[2,256,8192,1]{1,2,3,0:T(8,128)(2,1)} %bitcast.144, bf16[1,256,128]{2,1,0:T(8,128)(2,1)S(1)} %bitcast.151, bf16[1,256,128]{2,1,0:T(8,128)(2,1)S(1)} %bitcast.149, bf16[2,128,128]{2,1,0:T(8,128)(2,1)S(1)} %get-tuple-element.22, bf16[2,128,128]{2,1,0:T(8,128)(2,1)S(1)} %get-tuple-element.21, ...), kind=kOutput, calls=%fused_computation.1 | convolution fusion | flops 2148073472 | bytes 25427968 | tf_op jit(solution)/shard_map/xsk,ysp->xykp/dot_general | solution.py:96
  581.6 10.0 %slice_subtract_fusion.1 = (f32[1,1,128,8192]{2,3,0,1:T(8,128)}, f32[1,1,128,8192]{2,3,0,1:T(8,128)}) fusion(f32[2,2,128,8192]{2,3,0,1:T(8,128)} %convolution_bitcast_fusion), kind=kLoop, calls=%fused_computation.29 | loop fusion | flops 2097152 | bytes 25165824 | tf_op jit(solution)/shard_map/sub | solution.py:97
  591.6 5.5 copy.80
  597.2 5.5 copy.81
  603.0 0.6 reduce_sum.59
  603.6 1.2 multiply_divide_fusion
  604.7 5.2 fusion.12
  (31 shorter events, 1.1 us)
Async XLA Ops:
  8.8 3.9 copy-start.3
  110.4 158.1 %all-to-all-start = ((bf16[2,128,512,32]{1,3,0,2:T(8,128)(2,1)}), bf16[2,128,512,32]{1,3,0,2:T(8,128)(2,1)}, u32[]{:S(2)}, u32[]{:S(2)}) async-start(bf16[2,128,512,32]{1,3,0,2:T(8,128)(2,1)} %copy.69), calls=%async_computation | async-start | bytes 16777216 | tf_op jit(solution)/shard_map/all_to_all | solution.py:56
  117.8 435.2 %all-reduce.3.cloned.1.call-start = ((), (), s32[]{:S(2)}) async-start(), calls=%async_computation.1 | async-start | bytes 1048576 | tf_op jit(solution)/shard_map/psum | solution.py:79
  277.8 5.9 slice-start
  277.8 5.9 slice-start.1
  290.5 93.6 %collective-permute-start = (bf16[2,128,32,256]{3,1,2,0:T(8,128)(2,1)}, bf16[2,128,32,256]{3,1,2,0:T(8,128)(2,1)}, u32[]{:S(2)}, u32[]{:S(2)}) collective-permute-start(bf16[2,128,32,256]{3,1,2,0:T(8,128)(2,1)} %pad_maximum_fusion.5), channel_id=1, source_target_pairs={{0,16},{16,0},{1,17},{17,1},{2,18},{18,2},{3,19},{19,3},{4,20},{20... | collective-permute-start | bytes 12582920 | tf_op jit(solution)/shard_map/ppermute | solution.py:14
  387.2 4.5 copy-start
  393.5 159.6 %copy-start.2 = (f32[2,256,128]{2,1,0:T(8,128)S(1)}, f32[2,256,128]{2,1,0:T(8,128)}, u32[]{:S(2)}) copy-start(f32[2,256,128]{2,1,0:T(8,128)} %param.13) | copy-start | bytes 786436
  591.6 11.0 %copy-start.1 = (f32[256,256]{1,0:T(8,128)S(1)}, f32[256,256]{1,0:T(8,128)}, u32[]{:S(2)}) copy-start(f32[256,256]{1,0:T(8,128)} %get-tuple-element.6) | copy-start | bytes 786436
Sparse Core Ops, SparseCore 0:
  393.6 159.3 all-reduce.2

commit v2 on v1

--- a/solution.py
+++ b/solution.py
@@ -1,8 +1,11 @@
+import functools
 import math
 
 import jax
 import jax.numpy as jnp
 from jax import lax
+from jax.experimental import pallas as pl
+from jax.experimental.pallas import tpu as pltpu
 from jax.sharding import PartitionSpec as P
 
 NROW = 512
@@ -25,8 +28,194 @@
     )
 
 
+MESH = pl.DeviceIdType.MESH
+
+
+def place(flat, pix_size):
+    return (flat // pix_size, lax.rem(flat, pix_size))
+
+
+def greet(me, total, pix_size):
+    barrier = pltpu.get_barrier_semaphore()
+
+    def hello(step, carry):
+        other = lax.rem(me + step, total)
+        pl.semaphore_signal(barrier, inc=1, device_id=place(other, pix_size), device_id_type=MESH)
+        return carry
+
+    lax.fori_loop(1, total, hello, 0)
+    pl.semaphore_wait(barrier, total - 1)
+
+
+def all_reduce(me, total, pix_size, part, landed, result, sems):
+    def scatter(step):
+        other = lax.rem(me + step, total)
+        return pltpu.make_async_remote_copy(
+            src_ref=part.at[other],
+            dst_ref=landed.at[step],
+            send_sem=sems.at[0, step],
+            recv_sem=sems.at[1, step],
+            device_id=place(other, pix_size),
+            device_id_type=MESH,
+        )
+
+    def gather(step):
+        other = lax.rem(me + step, total)
+        return pltpu.make_async_remote_copy(
+            src_ref=result.at[me],
+            dst_ref=result.at[me],
+            send_sem=sems.at[2, step],
+            recv_sem=sems.at[3, step],
+            device_id=place(other, pix_size),
+            device_id_type=MESH,
+        )
+
+    def start_scatter(step, carry):
+        scatter(step).start()
+        return carry
+
+    def add_one(step, sum_so_far):
+        scatter(step).wait_recv()
+        return sum_so_far + landed[step]
+
+    def start_gather(step, carry):
+        gather(step).start()
+        return carry
+
+    def finish(step, carry):
+        scatter(step).wait_send()
+        gather(step).wait_send()
+        source = lax.rem(me - step + total, total)
+        pltpu.make_async_remote_copy(
+            src_ref=result.at[me],
+            dst_ref=result.at[source],
+            send_sem=sems.at[2, step],
+            recv_sem=sems.at[3, step],
+            device_id=place(source, pix_size),
+            device_id_type=MESH,
+        ).wait_recv()
+        return carry
+
+    lax.fori_loop(1, total, start_scatter, 0)
+    result[me] = lax.fori_loop(1, total, add_one, part[me])
+    lax.fori_loop(1, total, start_gather, 0)
+    lax.fori_loop(1, total, finish, 0)
+
+
+def reduce_kernel(grp_size, pix_size, part, result, landed, sems):
+    total = grp_size * pix_size
+    me = lax.axis_index("grp") * pix_size + lax.axis_index("pix")
+    greet(me, total, pix_size)
+    all_reduce(me, total, pix_size, part, landed, result, sems)
+
+
+def sum_over_devices(packed):
+    grp_size, pix_size = lax.axis_size("grp"), lax.axis_size("pix")
+    total = grp_size * pix_size
+    rows, columns = packed.shape
+    shape = (total, rows // total, columns)
+    out = pl.pallas_call(
+        functools.partial(reduce_kernel, grp_size, pix_size),
+        out_shape=jax.ShapeDtypeStruct(shape, jnp.float32),
+        in_specs=[pl.BlockSpec(memory_space=pltpu.VMEM)],
+        out_specs=pl.BlockSpec(memory_space=pltpu.VMEM),
+        scratch_shapes=[pltpu.VMEM(shape, jnp.float32), pltpu.SemaphoreType.DMA((4, total))],
+        compiler_params=pltpu.CompilerParams(collective_id=0, has_side_effects=True),
+    )(packed.reshape(shape))
+    return out.reshape(rows, columns)
+
+
+def pack_gram(real, imag):
+    size = real.shape[0]
+    row = lax.broadcasted_iota(jnp.int32, (size, size), 0)
+    column = lax.broadcasted_iota(jnp.int32, (size, size), 1)
+    return jnp.where(row <= column, real, imag)
+
+
+def modes_kernel(packed, start, group, owned, modes, power, weights, inverse):
+    highest = lax.Precision.HIGHEST
+    size = packed.shape[0]
+    rank = start.shape[0]
+
+    @pl.when(pl.program_id(0) == 0)
+    def _():
+        values = packed[...]
+        row = lax.broadcasted_iota(jnp.int32, (size, size), 0)
+        column = lax.broadcasted_iota(jnp.int32, (size, size), 1)
+        turned = values.T
+        real = jnp.where(row <= column, values, turned)
+        imag = jnp.where(row > column, values, jnp.where(row < column, -turned, 0.0))
+        gram = jnp.concatenate(
+            [jnp.concatenate([real, -imag], axis=1), jnp.concatenate([imag, real], axis=1)], axis=0
+        )
+        basis = start[...]
+        for _ in range(STEPS):
+            image = jnp.dot(basis, gram, precision=highest, preferred_element_type=jnp.float32)
+            basis = image / jnp.sqrt(jnp.sum(image * image, axis=1, keepdims=True) + 1e-06)
+        rounded = basis.astype(jnp.bfloat16)
+        coeff = rounded.astype(jnp.float32)
+        weighted = jnp.dot(coeff, gram, precision=highest, preferred_element_type=jnp.float32)
+        energy = jnp.sum(coeff * weighted, axis=1, keepdims=True)
+        trace = jnp.sum(jnp.where(row == column, values, 0.0))
+        power[...] = energy * size / trace
+        scale = lax.rsqrt(energy / (NROW * NCOL) + 1e-06)
+        inverse[...] = jnp.concatenate([scale, scale], axis=0)
+        half = size // 2
+        swap = group[0] == 1
+
+        def local_order(block):
+            return jnp.where(swap, jnp.concatenate([block[:, half:], block[:, :half]], axis=1), block)
+
+        real_part = local_order(coeff[:, :size])
+        imag_part = local_order(coeff[:, size:])
+        weights[...] = jnp.concatenate(
+            [
+                jnp.concatenate([real_part, -imag_part], axis=1),
+                jnp.concatenate([imag_part, real_part], axis=1),
+            ],
+            axis=0,
+        ).astype(jnp.bfloat16)
+
+    for step in range(owned.shape[1]):
+        block = jnp.concatenate([owned[0, step], owned[1, step]], axis=0)
+        product = jnp.dot(weights[...], block, preferred_element_type=jnp.float32) * inverse[...]
+        product = product.astype(jnp.bfloat16)
+        modes[0, step] = product[:rank]
+        modes[1, step] = product[rank:]
+
+
+def make_modes(packed, start_basis, group_index, owned):
+    _, count, slots, pixels = owned.shape
+    rank = start_basis.shape[2]
+    tile = math.gcd(count, 8)
+    start = jnp.concatenate([start_basis[0].T, start_basis[1].T], axis=1)
+    modes, power = pl.pallas_call(
+        modes_kernel,
+        grid=(count // tile,),
+        out_shape=(
+            jax.ShapeDtypeStruct((2, count, rank, pixels), jnp.bfloat16),
+            jax.ShapeDtypeStruct((rank, 1), jnp.float32),
+        ),
+        in_specs=[
+            pl.BlockSpec((slots, slots), lambda i: (0, 0)),
+            pl.BlockSpec((rank, 2 * slots), lambda i: (0, 0)),
+            pl.BlockSpec(memory_space=pltpu.SMEM),
+            pl.BlockSpec((2, tile, slots, pixels), lambda i: (0, i, 0, 0)),
+        ],
+        out_specs=(
+            pl.BlockSpec((2, tile, rank, pixels), lambda i: (0, i, 0, 0)),
+            pl.BlockSpec((rank, 1), lambda i: (0, 0)),
+        ),
+        scratch_shapes=[
+            pltpu.VMEM((2 * rank, 2 * slots), jnp.bfloat16),
+            pltpu.VMEM((2 * rank, 1), jnp.float32),
+        ],
+        compiler_params=pltpu.CompilerParams(vmem_limit_bytes=32 * 1024 * 1024),
+    )(packed, start, group_index.reshape(1), owned)
+    return modes, power.reshape(rank)
+
+
 def local(fields, lens_phase, occupancy, focus_scale, assignment, start_basis):
-    highest = lax.Precision.HIGHEST
     local_fields = fields[0]
     modes = local_fields.shape[1]
     group_index = lax.axis_index("grp")
@@ -73,43 +262,18 @@
     local_re = blocks[0, 0] + blocks[1, 1]
     local_im = blocks[0, 1] - blocks[1, 0]
 
-    def ordered(block):
-        return jnp.where(group_index == 0, block, jnp.roll(block, (modes, modes), (0, 1)))
-
-    gram_re, gram_im = lax.psum((ordered(local_re), ordered(local_im)), ("grp", "pix"))
-    basis_re = start_basis[0]
-    basis_im = start_basis[1]
-    for iteration in range(STEPS):
-        image_re = jnp.dot(gram_re, basis_re, precision=highest) - jnp.dot(
-            gram_im, basis_im, precision=highest
-        )
-        image_im = jnp.dot(gram_re, basis_im, precision=highest) + jnp.dot(
-            gram_im, basis_re, precision=highest
-        )
-        column_norm = jnp.sqrt(jnp.sum(image_re * image_re + image_im * image_im, axis=0) + 1e-06)
-        basis_re = image_re / column_norm[None, :]
-        basis_im = image_im / column_norm[None, :]
-    rounded = jnp.stack([basis_re, basis_im]).astype(jnp.bfloat16)
-    rank = rounded.shape[2]
-    local_rounded = jnp.where(group_index == 0, rounded, jnp.roll(rounded, modes, 1))
-    owned_flat = owned.reshape(2, stack_size, -1)
-    products = jnp.einsum("xsk,ysp->xykp", local_rounded, owned_flat, preferred_element_type=jnp.float32)
-    mode_re = products[0, 0] - products[1, 1]
-    mode_im = products[0, 1] + products[1, 0]
-    coeff_re = rounded[0].astype(jnp.float32)
-    coeff_im = rounded[1].astype(jnp.float32)
-    weighted_re = jnp.dot(gram_re, coeff_re, precision=highest) - jnp.dot(
-        gram_im, coeff_im, precision=highest
+    packed = jnp.where(
+        group_index == 0,
+        pack_gram(local_re, local_im),
+        pack_gram(
+            jnp.roll(local_re, (modes, modes), (0, 1)), jnp.roll(local_im, (modes, modes), (0, 1))
+        ),
     )
-    weighted_im = jnp.dot(gram_re, coeff_im, precision=highest) + jnp.dot(
-        gram_im, coeff_re, precision=highest
+    packed = sum_over_devices(packed)
+    coherent_modes, relative_power = make_modes(
+        packed, start_basis, group_index, jnp.swapaxes(owned, 1, 2)
     )
-    energy = jnp.sum(coeff_re * weighted_re + coeff_im * weighted_im, axis=0)
-    trace = jnp.sum(jnp.diagonal(gram_re))
-    relative_power = energy * stack_size / trace
-    inverse = lax.rsqrt(energy / (NROW * NCOL) + 1e-06)
-    coherent_modes = (jnp.stack([mode_re, mode_im]) * inverse[None, :, None]).astype(jnp.bfloat16)
-    return (coherent_modes.reshape(2, rank, owned.shape[2], owned.shape[3]), relative_power)
+    return (jnp.swapaxes(coherent_modes, 1, 2), relative_power)
 
 
 def solution(mesh):

time: 622 us -> 459 us (0.74)
  waiting for transfers between devices: 368 us -> 224 us
  Pallas kernels: 0 us -> 59.5 us
  matrix products: 78.6 us -> 51.9 us
  local copies, waits for them, and re-layouts: 51.7 us -> 30.5 us
  other arithmetic: 94.8 us -> 77.9 us
  between operations: 14.6 us -> 1.51 us
    psum x1 -> x0, waiting for transfers between devices: 147 us -> none  [local(): lax.psum((ordered(local_re), ordered(local_im)), ('grp', 'pix'))]
    pallas_call x0 -> x2, Pallas kernels: none -> 59.5 us  [the longest x1 53.4 us: sum_over_devices(): pl.pallas_call(functools.partial(reduce_kernel, grp_size, pix_size), out_...]
    dot_general x13 -> x0, matrix products: 26.1 us -> none  [the longest x1 11.5 us: local(): jnp.einsum('xsk,ysp->xykp', local_rounded, owned_flat, preferred_element_...]
    concatenate x1 -> x0, local copies, waits for them, and re-layouts: 12.2 us -> none  [local(): owned = jnp.concatenate([row_transform(0), partner], axis=1)]
    sub x1 -> x0, other arithmetic: 10 us -> none  [local(): mode_re = products[0, 0] - products[1, 1]]
    another operation x5 -> x4, other arithmetic: 55 us -> 54.8 us
  transfers between devices with their start and end apart: 3 -> 2, of which waited for: 3 -> 2; matrix products, arithmetic and copies ran while one was open for 6% -> 4% of each run, Pallas kernels for 0% -> 0%
where the time goes in v2:
time: 459 us; the launch traced here: 455 us
  waiting for transfers between devices  224 us (49%)
  other arithmetic  77.9 us (17%)
  Pallas kernels  59.5 us (13%)
  matrix products  51.9 us (11%)
  local copies, waits for them, and re-layouts  30.5 us (7%)
  starting transfers between devices  9.15 us (2%)
    all_to_all x1, waiting for transfers between devices, local(): lax.all_to_all(across, 'pix', split_axis=2, concat_axis=3, tiled=True)  142 us
    ppermute x1, waiting for transfers between devices, partner_2(): lax.ppermute(array, axis, [(i, i ^ 1 << apart) for i in range(lax.axis_si...  81.8 us
    another operation x4, other arithmetic  54.8 us
    pallas_call x1, Pallas kernels, sum_over_devices(): pl.pallas_call(functools.partial(reduce_kernel, grp_size, pix_size), out_...  53.4 us
    dot_general x1, matrix products, local(): jnp.einsum('zmrc,ck->zmkr', phased, sin_cols, preferred_element_type=jnp....  14.2 us
    dot_general x1, matrix products, local(): jnp.einsum('zmrc,ck->zmkr', phased, cos_cols, preferred_element_type=jnp....  14 us
    another operation x1, local copies, waits for them, and re-layouts, local(): jnp.stack([col_cos[0] + col_sin[1], col_cos[1] - col_sin[0]])  12 us
    all_to_all x1, local copies, waits for them, and re-layouts, local(): lax.all_to_all(across, 'pix', split_axis=2, concat_axis=3, tiled=True)  9.23 us
  transfers between devices with their start and end apart: 2, of which 2 were waited for; matrix products, arithmetic and copies ran while one was open for 4% of the time, Pallas kernels for 0%

profile of v2, /device:TPU:0, one launch (start us, length us, event | category | flops | bytes accessed | tf_op | source)
XLA Modules:
  0.0 454.6 jit_solution(207132439468257199)
XLA Ops:
  0.6 0.8 dynamic_slice.6
  1.4 0.9 select_reduce_fusion.1
  2.3 0.0 copy-start.3
  2.3 3.8 fusion.59
  6.1 0.0 copy-done.3
  6.1 37.5 %fusion.6 = (bf16[1,128,32,512]{3,1,2,0:T(8,128)(2,1)S(1)}, bf16[1,128,32,512]{3,1,2,0:T(8,128)(2,1)S(1)}) fusion(f32[32,512]{1,0:T(8,128)S(1)} %copy-done.3, f32[128]{0:T(128)S(1)} %get-tuple-element.18, f32[128]{0:T(128)S(1)} %sqrt.7, bf16[1,1,128,32,512]{4,3,2,1,0:T(8,128)(2,1)S(1)} %get-tuple-element.28, ...), kind=kLoop, calls=%fused_computation.8 | loop fusion | flops 27262976 | bytes 16843776 | tf_op jit(solution)/shard_map/convert.8
  43.6 14.0 %convolution_bitcast_fusion.1 = f32[2,128,512,32]{1,2,3,0:T(8,128)} fusion(bf16[1,128,32,512]{3,1,2,0:T(8,128)(2,1)S(1)} %get-tuple-element.26, bf16[1,128,32,512]{3,1,2,0:T(8,128)(2,1)S(1)} %get-tuple-element.25), kind=kOutput, calls=%fused_computation.23 | convolution fusion | flops 4315938816 | bytes 25165824 | tf_op jit(solution)/shard_map/zmrc,ck->zmkr/dot_general | solution.py:240
  57.6 14.2 %convolution_bitcast_fusion = f32[2,128,512,32]{1,2,3,0:T(8,128)} fusion(bf16[1,128,32,512]{3,1,2,0:T(8,128)(2,1)S(1)} %get-tuple-element.26, bf16[1,128,32,512]{3,1,2,0:T(8,128)(2,1)S(1)} %get-tuple-element.25), kind=kOutput, calls=%fused_computation.22 | convolution fusion | flops 4315938816 | bytes 25165824 | tf_op jit(solution)/shard_map/zmrc,ck->zmkr/dot_general | solution.py:241
  71.8 13.9 %fusion.11 = (bf16[1,128,512,32]{1,2,3,0:T(8,128)(2,1)S(1)}, bf16[1,128,512,32]{1,2,3,0:T(8,128)(2,1)}) fusion(f32[2,128,512,32]{1,2,3,0:T(8,128)} %convolution_bitcast_fusion, f32[2,128,512,32]{1,2,3,0:T(8,128)} %convolution_bitcast_fusion.1), kind=kLoop, calls=%fused_computation.15 | loop fusion | flops 8388608 | bytes 41943040 | tf_op jit(solution)/shard_map/convert.6
  85.7 6.2 %pad_maximum_fusion.1 = bf16[2,128,512,32]{1,2,3,0:T(8,128)(2,1)} fusion(bf16[1,128,512,32]{1,2,3,0:T(8,128)(2,1)} %get-tuple-element.20, bf16[1,128,512,32]{1,2,3,0:T(8,128)(2,1)S(1)} %get-tuple-element.19), kind=kLoop, calls=%fused_computation.17 | loop fusion | flops 4194304 | bytes 16777216 | tf_op jit(solution)/shard_map/stack | solution.py:242
  91.9 12.0 %copy.66 = bf16[2,128,512,32]{1,3,0,2:T(8,128)(2,1)} copy(bf16[2,128,512,32]{1,2,3,0:T(8,128)(2,1)} %pad_maximum_fusion.1) | data formatting | bytes 16777216 | tf_op jit(solution)/shard_map/stack | solution.py:242
  103.9 7.7 %all-to-all-start = ((bf16[2,128,512,32]{1,3,0,2:T(8,128)(2,1)}), bf16[2,128,512,32]{1,3,0,2:T(8,128)(2,1)}, u32[]{:S(2)}, u32[]{:S(2)}) async-start(bf16[2,128,512,32]{1,3,0,2:T(8,128)(2,1)} %copy.66), calls=%async_computation | async-start | bytes 16777216 | tf_op jit(solution)/shard_map/all_to_all | solution.py:245
  111.6 4.0 multiply_convert_fusion
  115.6 4.0 multiply_convert_fusion.1
  119.6 0.4 fusion.31
  120.0 142.2 %all-to-all-done = bf16[2,128,512,32]{1,3,0,2:T(8,128)(2,1)} async-done(((bf16[2,128,512,32]{1,3,0,2:T(8,128)(2,1)}), bf16[2,128,512,32]{1,3,0,2:T(8,128)(2,1)}, u32[]{:S(2)}, u32[]{:S(2)}) %all-to-all-start) | async-done | bytes 8388640 | tf_op jit(solution)/shard_map/all_to_all | solution.py:245
  262.2 9.2 %copy.68 = bf16[2,128,32,16,32]{1,4,3,2,0:T(8,128)(2,1)} copy(bf16[2,128,32,16,32]{1,4,0,2,3:T(8,128)(2,1)} %bitcast.10) | data formatting | bytes 16777216 | tf_op jit(solution)/shard_map/all_to_all | solution.py:245
  271.5 5.9 %fusion.36 = f32[2,128,32,256]{3,1,2,0:T(8,128)S(1)} fusion(bf16[2,128,32,512]{1,3,2,0:T(8,128)(2,1)} %bitcast.105, bf16[512,512]{1,0:T(8,128)(2,1)S(1)} %get-tuple-element.38), kind=kOutput, calls=%fused_computation.61 | convolution fusion | flops 2147483648 | bytes 17039360 | tf_op jit(solution)/shard_map/dot_general | solution.py:253
  277.4 0.0 slice-done
  277.4 0.0 slice-done.1
  277.4 2.4 fusion.35
  279.8 1.8 fusion.16
  281.6 0.0 copy-start.2
  281.7 2.4 pad_maximum_fusion.5
  284.0 1.5 collective-permute-start
  285.5 0.0 copy-done.2
  285.6 0.1 copy.95
  285.7 0.1 copy.96
  285.8 0.0 slice-start.2
  285.8 0.0 slice-start.3
  285.8 5.9 %fusion.37 = f32[2,128,32,256]{3,1,2,0:T(8,128)S(1)} fusion(bf16[2,128,32,512]{1,3,2,0:T(8,128)(2,1)} %bitcast.106, bf16[512,512]{1,0:T(8,128)(2,1)S(1)} %get-tuple-element.37), kind=kOutput, calls=%fused_computation.63 | convolution fusion | flops 2147483648 | bytes 17039360 | tf_op jit(solution)/shard_map/dot_general | solution.py:254
  291.7 0.0 slice-done.2
  291.8 0.0 slice-done.3
  291.8 2.4 fusion.38
  294.2 1.6 fusion.18
  295.8 0.0 copy-start.1
  295.8 81.8 %collective-permute-done = bf16[2,128,32,256]{3,1,2,0:T(8,128)(2,1)} collective-permute-done((bf16[2,128,32,256]{3,1,2,0:T(8,128)(2,1)}, bf16[2,128,32,256]{3,1,2,0:T(8,128)(2,1)}, u32[]{:S(2)}, u32[]{:S(2)}) %collective-permute-start) | collective-permute-done | bytes 4194336 | tf_op jit(solution)/shard_map/ppermute | solution.py:17
  377.6 7.1 %fusion.20 = f32[2,2,256,256]{3,2,0,1:T(8,128)S(1)} fusion(bf16[2,128,32,256]{3,1,2,0:T(8,128)(2,1)} %collective-permute-done, bf16[1,128,32,256]{3,1,2,0:T(8,128)(2,1)S(1)} %get-tuple-element.22, bf16[1,128,32,256]{3,1,2,0:T(8,128)(2,1)S(1)} %get-tuple-element.21), kind=kOutput, calls=%fused_computation.39 | convolution fusion | flops 4345298944 | bytes 9437184 | tf_op jit(solution)/shard_map/xap,ybp->xyab/dot_general | solution.py:261
  384.7 0.0 copy-done.1
  384.7 0.1 slice_subtract_fusion.3
  385.0 0.8 fusion.39.part
  385.8 53.4 %shard_map.77 = f32[32,8,256]{2,1,0:T(8,128)} custom-call(f32[32,8,256]{2,1,0:T(8,128)} %fusion.39.part), custom_call_target="tpu_custom_call" | custom-call | tf_op jit(solution)/shard_map/pallas_call | solution.py:117
  439.1 0.0 copy-start
  439.2 3.8 fusion.19.owned
  442.9 0.0 copy-done
  442.9 6.1 %shard_map.78 = (bf16[2,32,128,256]{3,2,1,0:T(8,128)(2,1)S(1)}, f32[128,1]{1,0:T(8,128)S(1)}) custom-call(f32[256,256]{1,0:T(8,128)S(1)} %bitcast.104, f32[128,512]{1,0:T(8,128)S(1)} %pad_maximum_fusion.7.start, s32[1]{0:T(128)} %bitcast.43.group, bf16[2,32,256,256]{3,2,1,0:T(8,128)(2,1)S(1)} %fusion.19.owned), custom_call_target="tpu_custom_call" | custom-call | tf_op jit(solution)/shard_map/pallas_call | solution.py:192
  449.1 4.4 copy.77
  453.5 0.6 reduce
  (14 shorter events, 0.1 us)
Async XLA Ops:
  2.3 3.9 copy-start.3
  103.9 158.3 %all-to-all-start = ((bf16[2,128,512,32]{1,3,0,2:T(8,128)(2,1)}), bf16[2,128,512,32]{1,3,0,2:T(8,128)(2,1)}, u32[]{:S(2)}, u32[]{:S(2)}) async-start(bf16[2,128,512,32]{1,3,0,2:T(8,128)(2,1)} %copy.66), calls=%async_computation | async-start | bytes 16777216 | tf_op jit(solution)/shard_map/all_to_all | solution.py:245
  271.5 5.9 %slice-start = ((s8[8388608]{0:T(1024)(128)(4,1)}), s8[4194304]{0:T(1024)(128)(4,1)S(1)}, s32[]{:S(2)}) async-start(s8[8388608]{0:T(1024)(128)(4,1)} %bitcast.107), calls=%async_computation.1 | async-start | bytes 8388608
  271.5 5.9 %slice-start.1 = ((s8[8388608]{0:T(1024)(128)(4,1)}), s8[4194304]{0:T(1024)(128)(4,1)S(1)}, s32[]{:S(2)}) async-start(s8[8388608]{0:T(1024)(128)(4,1)} %bitcast.107), calls=%async_computation.2 | async-start | bytes 8388608
  281.6 3.9 copy-start.2
  284.0 93.6 %collective-permute-start = (bf16[2,128,32,256]{3,1,2,0:T(8,128)(2,1)}, bf16[2,128,32,256]{3,1,2,0:T(8,128)(2,1)}, u32[]{:S(2)}, u32[]{:S(2)}) collective-permute-start(bf16[2,128,32,256]{3,1,2,0:T(8,128)(2,1)} %pad_maximum_fusion.5), channel_id=1, source_target_pairs={{0,16},{16,0},{1,17},{17,1},{2,18},{18,2},{3,19},{19,3},{4,20},{20... | collective-permute-start | bytes 12582920 | tf_op jit(solution)/shard_map/ppermute | solution.py:17
  285.8 6.0 %slice-start.2 = ((s8[8388608]{0:T(1024)(128)(4,1)}), s8[4194304]{0:T(1024)(128)(4,1)S(1)}, s32[]{:S(2)}) async-start(s8[8388608]{0:T(1024)(128)(4,1)} %bitcast.110), calls=%async_computation.3 | async-start | bytes 8388608
  285.8 5.9 %slice-start.3 = ((s8[8388608]{0:T(1024)(128)(4,1)}), s8[4194304]{0:T(1024)(128)(4,1)S(1)}, s32[]{:S(2)}) async-start(s8[8388608]{0:T(1024)(128)(4,1)} %bitcast.110), calls=%async_computation.4 | async-start | bytes 8388608
  295.8 89.0 %copy-start.1 = (bf16[1,128,32,256]{3,1,2,0:T(8,128)(2,1)}, bf16[1,128,32,256]{3,1,2,0:T(8,128)(2,1)S(1)}, u32[]{:S(2)}) copy-start(bf16[1,128,32,256]{3,1,2,0:T(8,128)(2,1)S(1)} %get-tuple-element.22) | copy-start | bytes 6291460
  439.1 3.8 copy-start
